TPU v7x, 512 devices: a whole 4x4x16 slice. The times are simulated.
512 devices in a mesh: gx: 32 (over z, core), gy: 16 (over y, x).
Axes of the slice: x: 4, y: 4, z: 16, core: 2. Of those that a mesh axis runs over, the one named last changes fastest.
Arguments:
- field: bfloat16 [512, 64, 48, 512], P('gx', None, 'gy'), may hold values from -450 to 450, as said below
- start_one: float32 [512, 128], replicated, may hold values from -6 to 6
- start_two: float32 [512, 128], replicated, may hold values from -6 to 6
Outputs:
- basis_one: float32 [512, 128], replicated
- basis_two: float32 [512, 128], replicated
- core: bfloat16 [128, 64, 48, 128], P(None, 'gx', 'gy')
Inputs may be any that keep to these rules, and one draw needn't show every extreme that they name: The field is random, with scales that vary smoothly along each mode, and may contain a few sharp spikes and smooth waves.
All inputs are finite; a program needn't handle non-finite values.
Results may differ from a plain program's by a relative error of at most 0.0075.
Values may be sent and summed in bfloat16 or wider, within the bound.
A program may use at most 64 MiB of HBM per device.

v0:
```python
import jax
import jax.numpy as jnp
from jax import lax
from jax.sharding import PartitionSpec as P

R = 128
ITERS = 2


def orth(block):
    for turn in range(2):
        inner = jnp.dot(block.T, block, precision=lax.Precision.HIGHEST)
        lower = jnp.linalg.cholesky(inner)
        block = lax.linalg.triangular_solve(
            lower, block, left_side=False, lower=True, transpose_a=True
        )
    return block


def leading(gram, start):
    basis = orth(start)
    for step in range(ITERS):
        basis = orth(jnp.dot(gram, basis, precision=lax.Precision.HIGHEST))
    return basis


def reduce_gram(partial_gram):
    return lax.psum(partial_gram, ("gx", "gy"))


def mode_basis(rows_first, start):
    partial_gram = lax.dot_general(
        rows_first, rows_first, (((1,), (1,)), ((), ())), preferred_element_type=jnp.float32
    )
    return leading(reduce_gram(partial_gram), start)


def local(field, start_one, start_two):
    local_two, size_three, local_four, size_one = field.shape
    flat_rows = field.reshape(-1, size_one)
    basis_one = mode_basis(flat_rows.T, start_one)
    narrow_one = basis_one.astype(jnp.bfloat16)
    core_one = jnp.dot(flat_rows, narrow_one, preferred_element_type=jnp.float32).astype(
        jnp.bfloat16
    )
    core_one = core_one.reshape(local_two, size_three, local_four, R)
    moved_core = lax.all_to_all(core_one, "gx", split_axis=1, concat_axis=0, tiled=True)
    whole_two, local_three = (moved_core.shape[0], moved_core.shape[1])
    flat_two = moved_core.reshape(whole_two, -1)
    basis_two = mode_basis(flat_two, start_two)
    narrow_two = basis_two.astype(jnp.bfloat16)
    projected = lax.dot_general(
        narrow_two, flat_two, (((0,), (0,)), ((), ())), preferred_element_type=jnp.float32
    )
    core = projected.astype(jnp.bfloat16).reshape(R, local_three, local_four, R)
    return (basis_one, basis_two, core)


def solution(mesh):
    placed = (P("gx", None, "gy", None), P(), P())
    return jax.shard_map(
        local,
        mesh=mesh,
        in_specs=placed,
        out_specs=(P(), P(), P(None, "gx", "gy", None)),
        check_vma=False,
    )
```

profile of v0, /device:TPU:1, one launch (start us, length us, event | category | flops | bytes accessed | tf_op | source)
XLA Modules:
  0.0 1230.7 jit_solution(16206858843879811838)
XLA Ops:
  7.2 5.8 convolution_bitcast_fusion
  13.1 4.6 copy.46
  18.4 11.7 cholesky.194
  30.8 0.7 fusion.3
  31.5 9.8 custom-call.16
  41.8 0.7 copy-done.3
  43.0 12.0 cholesky.205
  55.7 0.7 fusion.4
  56.3 9.8 custom-call.17
  66.2 7.5 reshape.30
  73.7 2.1 convolution_bitcast_fusion.11
  75.8 410.5 %all-reduce.3.cloned.1.call-done = f32[512,512]{1,0:T(8,128)} async-done(((f32[512,512]{1,0:T(8,128)}), f32[512,512]{1,0:T(8,128)}) %all-reduce.3.cloned.1.call-update) | async-done | bytes 1048592 | tf_op jit(solution)/shard_map/psum | solution.py:28
  486.2 2.3 fusion.51
  488.5 0.7 copy-done.7
  490.5 12.5 %cholesky.216 = f32[128,128]{1,0:T(8,128)S(1)} custom-call(f32[128,128]{1,0:T(8,128)} %fusion.34), custom_call_target="Cholesky" | custom-call | tf_op jit(solution)/shard_map/jit(cholesky)/cholesky | solution.py:13
  503.8 0.7 fusion.5
  504.4 9.8 custom-call.18
  514.2 1.4 convolution_bitcast_fusion.10
  515.6 0.7 copy-done.4
  517.4 12.7 %cholesky.227 = f32[128,128]{1,0:T(8,128)S(1)} custom-call(f32[128,128]{1,0:T(8,128)} %fusion.32), custom_call_target="Cholesky" | custom-call | tf_op jit(solution)/shard_map/jit(cholesky)/cholesky | solution.py:13
  530.8 0.7 fusion.6
  531.5 9.8 custom-call.19
  541.3 1.4 convolution_bitcast_fusion.9
  542.7 2.2 fusion.54
  544.9 0.7 copy-done.6
  547.0 12.5 %cholesky.238 = f32[128,128]{1,0:T(8,128)S(1)} custom-call(f32[128,128]{1,0:T(8,128)} %fusion.30), custom_call_target="Cholesky" | custom-call | tf_op jit(solution)/shard_map/jit(cholesky)/cholesky | solution.py:13
  560.2 0.7 fusion.7
  560.8 9.8 custom-call.20
  570.7 1.4 convolution_bitcast_fusion.8
  572.0 0.7 copy-done.5
  573.9 12.7 %cholesky.249 = f32[128,128]{1,0:T(8,128)S(1)} custom-call(f32[128,128]{1,0:T(8,128)} %fusion.28), custom_call_target="Cholesky" | custom-call | tf_op jit(solution)/shard_map/jit(cholesky)/cholesky | solution.py:13
  587.3 0.7 fusion.8
  588.0 9.8 custom-call.21
  597.8 1.4 convolution_bitcast_fusion.7
  599.2 0.7 copy-done.9
  599.9 2.0 fusion
  601.9 1.5 copy.47
  603.8 1.8 copy.48
  605.6 10.1 all-to-all-start
  616.9 11.7 cholesky.260
  629.3 0.7 fusion.9
  630.0 9.8 custom-call.22
  640.7 11.7 cholesky.271
  652.5 7.9 all-to-all-done
  660.9 0.9 reshape.32
  661.8 1.6 fusion.57
  664.1 0.7 fusion.10
  664.8 9.8 custom-call.23
  675.0 0.8 copy.57
  675.9 446.1 %all-reduce.5.cloned.1.call-done = f32[512,512]{1,0:T(8,128)} async-done(((f32[512,512]{1,0:T(8,128)}), f32[512,512]{1,0:T(8,128)}) %all-reduce.5.cloned.1.call-update) | async-done | bytes 1048592 | tf_op jit(solution)/shard_map/psum | solution.py:28
  1122.0 2.3 fusion.60
  1125.0 11.7 cholesky.282
  1137.4 0.7 fusion.11
  1138.0 9.8 custom-call.24
  1148.8 11.9 cholesky.293
  1161.3 0.7 fusion.12
  1162.0 9.8 custom-call.25
  1172.3 1.0 fusion.63
  1174.0 11.7 cholesky.304
  1187.0 10.0 custom-call.26
  1198.0 11.7 cholesky.315
  1211.0 9.8 custom-call.27
  1221.6 0.8 copy.58
  1222.6 0.8 copy.59
  (93 shorter events, 23.8 us)
Async XLA Ops:
  7.2 10.6 copy-start
  7.2 5.9 copy-start.1
  7.2 479.0 %all-reduce.3.cloned.1.call-start = ((), (), s32[]{:S(2)}) async-start(), calls=%async_computation.1 | async-start | bytes 2097152 | tf_op jit(solution)/shard_map/psum | solution.py:28
  41.7 0.7 copy-start.3
  488.5 0.7 copy-start.7
  515.6 0.7 copy-start.4
  544.9 0.7 copy-start.6
  572.0 0.7 copy-start.5
  599.2 0.7 copy-start.9
  601.9 14.3 %copy-start.8 = (f32[512,128]{1,0:T(8,128)S(1)}, f32[512,128]{1,0:T(8,128)}, u32[]{:S(2)}) copy-start(f32[512,128]{1,0:T(8,128)} %param.8) | copy-start | bytes 786436
  605.6 54.8 %all-to-all-start = ((bf16[16,64,3,128]{3,0,2,1:T(8,128)(2,1)}), bf16[16,64,3,128]{3,0,2,1:T(8,128)(2,1)S(1)}, u32[]{:S(2)}, u32[]{:S(2)}) async-start(bf16[16,64,3,128]{3,0,2,1:T(8,128)(2,1)} %copy.48), calls=%async_computation | async-start | bytes 1572864 | tf_op jit(solution)/shard_map/all_to_all | solution.py:47
  615.7 506.2 %all-reduce.5.cloned.1.call-start = ((), (), s32[]{:S(2)}) async-start(), calls=%async_computation.2 | async-start | bytes 2097152 | tf_op jit(solution)/shard_map/psum | solution.py:28
  660.9 14.1 %copy-start.10 = (f32[512,128]{0,1:T(8,128)S(1)}, f32[512,128]{0,1:T(8,128)}, u32[]{:S(2)}) copy-start(f32[512,128]{0,1:T(8,128)} %copy-done.9) | copy-start | bytes 786436
  1122.0 50.3 %copy-start.2 = (f32[512,512]{1,0:T(8,128)S(1)}, f32[512,512]{1,0:T(8,128)}, u32[]{:S(2)}) copy-start(f32[512,512]{1,0:T(8,128)} %all-reduce.5.cloned.1.call-done) | copy-start | bytes 3145732
Sparse Core Ops, SparseCore 0:
  13.5 472.6 all-reduce.2
  663.6 458.2 all-reduce.4
where the time goes:
time: 1240 us; the launch traced here: 1230 us
  waiting for transfers between devices  865 us (70%)
  other arithmetic  281 us (23%)
  matrix products  33.8 us (3%)
  local copies, waits for them, and re-layouts  25.2 us (2%)
  between operations  15.2 us (1%)
    psum x2, waiting for transfers between devices, reduce_gram(): return lax.psum(partial_gram, ('gx', 'gy'))  857 us
    another operation x36, other arithmetic, orth(): lower = jnp.linalg.cholesky(inner)  153 us
    another operation x24, other arithmetic, orth(): lax.linalg.triangular_solve(lower, block, left_side=False, lower=True, tr...  126 us
  transfers between devices with their start and end apart: 3, of which 3 were waited for; matrix products, arithmetic and copies ran while one was open for 9% of the time, Pallas kernels for 0%

commit v1 on v0

v1 whole, which is shorter than its diff:
```python
import functools

import jax
import jax.numpy as jnp
from jax import lax
from jax.experimental import pallas as pl
from jax.experimental.pallas import tpu as pltpu
from jax.sharding import PartitionSpec as P

F32 = jnp.float32
BF16 = jnp.bfloat16
HIGHEST = lax.Precision.HIGHEST
MESH = pl.DeviceIdType.MESH
N = 512
R = 128
NX = 32
NY = 16
BLOCKS = [(a, b) for a in range(4) for b in range(a, 4)]
TILES = 160
PER = TILES // NY
GAP = 3
VMEM_LIMIT = 48 * 1024 * 1024


def tree_sum(terms):
    while len(terms) > 1:
        terms = [
            terms[i] + terms[i + 1] if i + 1 < len(terms) else terms[i]
            for i in range(0, len(terms), 2)
        ]
    return terms[0]


def factor_inverse(gram):
    width = 16
    parts = width // 8
    row = lax.broadcasted_iota(jnp.int32, (R, R), 0)
    column = lax.broadcasted_iota(jnp.int32, (R, R), 1)
    diagonal = jnp.where(row == column, gram, 0.0)
    scale_rows = lax.rsqrt(jnp.sum(diagonal, axis=1, keepdims=True))
    scale_columns = lax.rsqrt(jnp.sum(diagonal, axis=0, keepdims=True))
    scaled = gram * scale_rows * scale_columns
    held = [scaled[8 * i : 8 * i + 8, :] for i in range(R // 8)]
    lane = lax.broadcasted_iota(jnp.int32, (8, R), 1)
    sub = lax.broadcasted_iota(jnp.int32, (8, R), 0)

    def along_lanes(x, l):
        return jnp.broadcast_to(x[:, l : l + 1], (8, R))

    def along_subs(x, s):
        return jnp.broadcast_to(x[s : s + 1, :], (8, R))

    out = []
    for k in range(R // width):
        base = k * width
        panel = [held[k * parts + t] for t in range(parts)]
        cols = [[along_lanes(panel[t], base + q) for t in range(parts)] for q in range(width)]
        panel = [
            jnp.where(lane == base + 8 * t + sub, panel[t] + 1.0, panel[t]) for t in range(parts)
        ]
        rows = []
        for j in range(width):
            tj, sj = divmod(j, 8)
            pivot = along_subs(cols[j][tj], sj)
            inverse = 1.0 / pivot
            pivot_row = along_subs(panel[tj], sj)
            kept = jnp.where(lane < base + j, pivot_row, jnp.where(lane == base + j, 1.0, 0.0))
            rows.append(kept * lax.rsqrt(pivot))
            factor = cols[j]
            pivot_row = pivot_row * inverse
            for t in range(parts):
                new = panel[t] - factor[t] * pivot_row
                panel[t] = jnp.where(sub == sj, pivot_row, new) if t == tj else new
            for q in range(j + 1, width):
                entry = along_subs(cols[q][tj], sj) * inverse
                for t in range(parts):
                    new = cols[q][t] - factor[t] * entry
                    cols[q][t] = jnp.where(sub == sj, entry, new) if t == tj else new
        for t in range(parts):
            block = rows[8 * t]
            for s in range(1, 8):
                block = jnp.where(sub >= s, rows[8 * t + s], block)
            out.append(block)
        spread = [along_subs(panel[q // 8], q % 8) for q in range(width)]
        for i in range((k + 1) * parts, R // 8):
            x = held[i]
            held[i] = x - tree_sum([along_lanes(x, base + q) * spread[q] for q in range(width)])
    return jnp.concatenate(out, axis=0) * scale_columns


def dot_tn(a, b, precision=None):
    return lax.dot_general(
        a, b, (((0,), (0,)), ((), ())), precision=precision, preferred_element_type=F32
    )


def dot_nt(a, b, precision=None):
    return lax.dot_general(
        a, b, (((1,), (1,)), ((), ())), precision=precision, preferred_element_type=F32
    )


def orth_pass(y_ref):
    y = y_ref[...]
    y_ref[...] = dot_nt(y, factor_inverse(dot_tn(y, y, HIGHEST)), HIGHEST)


def basis_chain(gram_ref, start_ref, y_ref):
    y_ref[...] = start_ref[...]

    def step(t, carry):
        @pl.when(jnp.logical_and(t >= 2, lax.rem(t, 2) == 0))
        def _():
            y_ref[...] = jnp.dot(
                gram_ref[...], y_ref[...], precision=HIGHEST, preferred_element_type=F32
            )

        orth_pass(y_ref)
        return carry

    lax.fori_loop(0, 6, step, 0)


def enter(gx, gy):
    barrier = pltpu.get_barrier_semaphore()

    def greet_y(d, carry):
        pl.semaphore_signal(
            barrier, inc=1, device_id=(gx, lax.rem(gy + d, NY)), device_id_type=MESH
        )
        return carry

    def greet_x(d, carry):
        pl.semaphore_signal(
            barrier, inc=1, device_id=(lax.rem(gx + d, NX), gy), device_id_type=MESH
        )
        return carry

    lax.fori_loop(1, NY, greet_y, 0)
    lax.fori_loop(1, NX, greet_x, 0)
    return barrier


def remote(src, dst, send, recv, device):
    return pltpu.make_async_remote_copy(
        src_ref=src,
        dst_ref=dst,
        send_sem=send,
        recv_sem=recv,
        device_id=device,
        device_id_type=MESH,
    )


def wait_bytes(ref, sem):
    pltpu.make_async_copy(ref, ref, sem).wait()


def sum_all(gx, gy, tiles, plane_in, line_out, line_in, piece, full, sems):
    s1, r1, s2, r2, s3, r3, s4, r4 = [sems.at[i] for i in range(8)]

    def send_plane(d, carry):
        to = lax.rem(gy + d, NY)
        remote(tiles.at[pl.ds(to * PER, PER)], plane_in.at[gy], s1, r1, (gx, to)).start()
        return carry

    lax.fori_loop(1, NY, send_plane, 0)
    plane_in[gy] = tiles[pl.ds(gy * PER, PER)]
    wait_bytes(plane_in.at[pl.ds(0, NY - 1)], r1)
    line_out[...] = tree_sum([plane_in[p] for p in range(NY)])

    for t in range(PER):
        owner = GAP * t

        @pl.when(gx != owner)
        def _():
            remote(line_out.at[t], line_in.at[gx], s2, r2, (owner, gy)).start()

        @pl.when(gx == owner)
        def _():
            line_in[gx] = line_out[t]

    mine = jnp.logical_and(lax.rem(gx, GAP) == 0, gx < GAP * PER)
    slot = lax.div(gx, GAP)

    @pl.when(mine)
    def _():
        wait_bytes(line_in.at[pl.ds(0, NX - 1)], r2)
        piece[slot] = tree_sum([line_in[p] for p in range(NX)])

        def send_line(d, carry):
            remote(
                piece.at[slot], piece.at[slot], s3, r3, (lax.rem(gx + d, NX), gy)
            ).start()
            return carry

        lax.fori_loop(1, NX, send_line, 0)
        wait_bytes(piece.at[pl.ds(0, PER - 1)], r3)

    @pl.when(jnp.logical_not(mine))
    def _():
        wait_bytes(piece, r3)

    def send_back(d, carry):
        to = lax.rem(gy + d, NY)
        remote(piece, full.at[pl.ds(gy * PER, PER)], s4, r4, (gx, to)).start()
        return carry

    lax.fori_loop(1, NY, send_back, 0)
    full[pl.ds(gy * PER, PER)] = piece[...]
    wait_bytes(full.at[pl.ds(0, TILES - PER)], r4)

    wait_bytes(tiles.at[pl.ds(0, TILES - PER)], s1)
    wait_bytes(full.at[pl.ds(0, TILES - PER)], s4)

    @pl.when(mine)
    def _():
        wait_bytes(line_out.at[pl.ds(0, PER - 1)], s2)
        wait_bytes(line_in.at[pl.ds(0, NX - 1)], s3)

    @pl.when(jnp.logical_not(mine))
    def _():
        wait_bytes(line_out, s2)


SUM_SCRATCH = [
    pltpu.VMEM((TILES, 8, R), F32),
    pltpu.VMEM((NY, PER, 8, R), F32),
    pltpu.VMEM((PER, 8, R), F32),
    pltpu.VMEM((NX, 8, R), F32),
    pltpu.VMEM((PER, 8, R), F32),
    pltpu.VMEM((TILES, 8, R), F32),
    pltpu.SemaphoreType.DMA((8,)),
]


def unpack(full, gram_ref):
    for index, (a, b) in enumerate(BLOCKS):
        block = full[pl.ds(16 * index, 16)].reshape(R, R)
        gram_ref[pl.ds(a * R, R), pl.ds(b * R, R)] = block
        if a != b:
            gram_ref[pl.ds(b * R, R), pl.ds(a * R, R)] = block.T


def gram_one_kernel(x_ref, gram_ref, tiles, plane_in, line_out, line_in, piece, full, sems):
    gx = lax.axis_index("gx")
    gy = lax.axis_index("gy")
    barrier = enter(gx, gy)
    for a in range(4):
        strip = dot_tn(x_ref[:, pl.ds(a * R, R)], x_ref[:, pl.ds(a * R, N - a * R)])
        for b in range(a, 4):
            tiles[pl.ds(16 * BLOCKS.index((a, b)), 16)] = strip[
                :, (b - a) * R : (b - a + 1) * R
            ].reshape(16, 8, R)
    pl.semaphore_wait(barrier, NX + NY - 2)
    sum_all(gx, gy, tiles, plane_in, line_out, line_in, piece, full, sems)
    unpack(full, gram_ref)


def gram_two_kernel(
    x_ref,
    narrow_ref,
    gram_ref,
    flat_ref,
    wide,
    out_slots,
    tiles,
    plane_in,
    line_out,
    line_in,
    piece,
    full,
    sems,
    move_sems,
):
    gx = lax.axis_index("gx")
    gy = lax.axis_index("gy")
    barrier = enter(gx, gy)
    narrow = narrow_ref[...]

    def project(i, carry):
        rows = pl.ds(pl.multiple_of(i * 192, 192), 192)
        wide[rows, :] = jnp.dot(x_ref[rows, :], narrow, preferred_element_type=F32)
        return carry

    lax.fori_loop(0, 16, project, 0)
    pl.semaphore_wait(barrier, NX + NY - 2)

    def regroup(d, carry):
        to = lax.rem(gx + d, NX)
        for k in range(3):
            for j in range(2):
                column = wide[pl.ds(k * 64 + to * 2 + j, 16, stride=192), :]
                out_slots[to, k * 2 + j] = column.astype(BF16)

        @pl.when(d < NX)
        def _():
            remote(
                out_slots.at[to], flat_ref.at[gx], move_sems.at[0], move_sems.at[1], (to, gy)
            ).start()

        return carry

    lax.fori_loop(1, NX + 1, regroup, 0)
    flat_ref[gx] = out_slots[gx]
    wait_bytes(flat_ref.at[pl.ds(0, NX - 1)], move_sems.at[1])
    wait_bytes(out_slots.at[pl.ds(0, NX - 1)], move_sems.at[0])
    for a in range(4):
        strip = None
        for c in range(6):
            left = flat_ref[pl.ds(8 * a, 8), c].reshape(R, R)
            right = flat_ref[pl.ds(8 * a, NX - 8 * a), c].reshape(N - a * R, R)
            part = dot_nt(left, right)
            strip = part if strip is None else strip + part
        for b in range(a, 4):
            tiles[pl.ds(16 * BLOCKS.index((a, b)), 16)] = strip[
                :, (b - a) * R : (b - a + 1) * R
            ].reshape(16, 8, R)
    sum_all(gx, gy, tiles, plane_in, line_out, line_in, piece, full, sems)
    unpack(full, gram_ref)


def chain_one_kernel(gram_ref, start_ref, basis_ref, narrow_ref):
    basis_chain(gram_ref, start_ref, basis_ref)
    narrow_ref[...] = basis_ref[...].astype(BF16)


def chain_two_kernel(gram_ref, start_ref, flat_ref, basis_ref, core_ref):
    basis_chain(gram_ref, start_ref, basis_ref)
    narrow = basis_ref[...].astype(BF16)
    for c in range(6):
        core_ref[c] = dot_tn(narrow, flat_ref[:, c].reshape(N, R)).astype(BF16)


def vmem(count):
    return [pl.BlockSpec(memory_space=pltpu.VMEM)] * count


def call(kernel, outs, inputs, scratch=(), collective=None):
    return pl.pallas_call(
        kernel,
        out_shape=[jax.ShapeDtypeStruct(shape, dtype) for shape, dtype in outs],
        in_specs=vmem(len(inputs)),
        out_specs=vmem(len(outs)),
        scratch_shapes=list(scratch),
        compiler_params=pltpu.CompilerParams(
            collective_id=collective,
            has_side_effects=collective is not None,
            vmem_limit_bytes=VMEM_LIMIT,
        ),
    )(*inputs)


def local(field, start_one, start_two):
    rows = field.transpose(0, 2, 1, 3).reshape(-1, N)
    (gram_one,) = call(gram_one_kernel, [((N, N), F32)], [rows], SUM_SCRATCH, 0)
    basis_one, narrow_one = call(
        chain_one_kernel, [((N, R), F32), ((N, R), BF16)], [gram_one, start_one]
    )
    gram_two, flat_two = call(
        gram_two_kernel,
        [((N, N), F32), ((NX, 6, 16, R), BF16)],
        [rows, narrow_one],
        [pltpu.VMEM((3072, R), F32), pltpu.VMEM((NX, 6, 16, R), BF16)]
        + SUM_SCRATCH
        + [pltpu.SemaphoreType.DMA((2,))],
        1,
    )
    basis_two, core = call(
        chain_two_kernel, [((N, R), F32), ((6, R, R), BF16)], [gram_two, start_two, flat_two]
    )
    core = core.reshape(3, 2, R, R).transpose(2, 1, 0, 3)
    return basis_one, basis_two, core


def solution(mesh):
    placed = (P("gx", None, "gy", None), P(), P())
    return jax.shard_map(
        local,
        mesh=mesh,
        in_specs=placed,
        out_specs=(P(), P(), P(None, "gx", "gy", None)),
        check_vma=False,
    )
```

time: 1240 us -> 198 us (0.16)
  waiting for transfers between devices: 865 us -> 0 us
  other arithmetic: 281 us -> 0 us
  Pallas kernels: 0 us -> 195 us
  matrix products: 33.8 us -> 0 us
  local copies, waits for them, and re-layouts: 25.2 us -> 2.78 us
  between operations: 15.2 us -> 0.68 us
    psum x2 -> x0, waiting for transfers between devices: 857 us -> none  [reduce_gram(): return lax.psum(partial_gram, ('gx', 'gy'))]
    another operation x60 -> x0, other arithmetic: 279 us -> none  [the longest x36 153 us: orth(): lower = jnp.linalg.cholesky(inner)]
    pallas_call x0 -> x4, Pallas kernels: none -> 195 us  [call(): pl.pallas_call(kernel, out_shape=[jax.ShapeDtypeStruct(shape, dtype) for...]
    dot_general x20 -> x0, matrix products: 23.3 us -> none  [the longest x4 7.76 us: leading(): basis = orth(jnp.dot(gram, basis, precision=lax.Precision.HIGHEST))]
  transfers between devices with their start and end apart: 3 -> 0, of which waited for: 3 -> 0; matrix products, arithmetic and copies ran while one was open for 9% -> 0% of each run, Pallas kernels for 0% -> 0%
where the time goes in v1:
time: 198 us
  Pallas kernels  195 us (98%)
  local copies, waits for them, and re-layouts  2.78 us (1%)
    pallas_call x4, Pallas kernels, call(): pl.pallas_call(kernel, out_shape=[jax.ShapeDtypeStruct(shape, dtype) for...  195 us

profile of v1, /device:TPU:1, one launch (start us, length us, event | category | flops | bytes accessed | tf_op | source)
XLA Modules:
  0.0 198.1 jit_solution(3147116744580532536)
XLA Ops:
  0.6 0.0 copy-start
  0.6 1.9 copy-done
  2.5 0.0 copy-start.2
  2.5 0.0 copy-start.1
  2.5 54.2 %shard_map.58.gram_ref = f32[512,512]{1,0:T(8,128)S(1)} custom-call(bf16[3072,512]{1,0:T(8,128)(2,1)S(1)} %bitcast.7), custom_call_target="tpu_custom_call" | custom-call | tf_op jit(solution)/shard_map/pallas_call | solution.py:340
  56.7 0.0 copy-done.2
  56.7 0.0 copy-start.3
  56.7 29.9 %shard_map.59 = (f32[512,128]{1,0:T(8,128)}, bf16[512,128]{1,0:T(8,128)(2,1)S(1)}) custom-call(f32[512,512]{1,0:T(8,128)S(1)} %shard_map.58.gram_ref, f32[512,128]{1,0:T(8,128)S(1)} %copy-done.2), custom_call_target="tpu_custom_call" | custom-call | tf_op jit(solution)/shard_map/pallas_call | solution.py:340
  86.6 0.0 copy-done.1
  86.6 80.6 %shard_map.60 = (f32[512,512]{1,0:T(8,128)S(1)}, bf16[32,6,16,128]{3,2,1,0:T(8,128)(2,1)S(1)}) custom-call(bf16[3072,512]{1,0:T(8,128)(2,1)S(1)} %bitcast.8, bf16[512,128]{1,0:T(8,128)(2,1)S(1)} %get-tuple-element.10.narrow_ref), custom_call_target="tpu_custom_call" | custom-call | tf_op jit(solution)/shard_map/pallas_call | solution.py:340
  167.3 0.0 copy-done.3
  167.3 29.9 %shard_map.61 = (f32[512,128]{1,0:T(8,128)}, bf16[6,128,128]{2,1,0:T(8,128)(2,1)S(1)}) custom-call(f32[512,512]{1,0:T(8,128)S(1)} %get-tuple-element.11.gram_ref, f32[512,128]{1,0:T(8,128)S(1)} %copy-done.3, bf16[32,6,16,128]{3,2,1,0:T(8,128)(2,1)S(1)} %get-tuple-element.12.flat_ref), custom_call_target="tpu_custom_call" | custom-call | tf_op jit(solution)/shard_map/pallas_call | solution.py:340
  197.2 0.9 copy.8
Async XLA Ops:
  0.6 1.9 copy-start
  2.5 54.2 %copy-start.2 = (f32[512,128]{1,0:T(8,128)S(1)}, f32[512,128]{1,0:T(8,128)}, u32[]{:S(2)}) copy-start(f32[512,128]{1,0:T(8,128)} %start_ref.2) | copy-start | bytes 786436
  2.5 84.1 %copy-start.1 = (bf16[16,64,3,512]{3,1,2,0:T(8,128)(2,1)S(1)}, bf16[16,64,3,512]{3,1,2,0:T(8,128)(2,1)}, u32[]{:S(2)}) copy-start(bf16[16,64,3,512]{3,1,2,0:T(8,128)(2,1)} %param.3) | copy-start | bytes 9437188
  56.7 110.6 %copy-start.3 = (f32[512,128]{1,0:T(8,128)S(1)}, f32[512,128]{1,0:T(8,128)}, u32[]{:S(2)}) copy-start(f32[512,128]{1,0:T(8,128)} %start_ref.3) | copy-start | bytes 786436

commit v2 on v1

v2 whole, which is shorter than its diff:
```python
import functools

import jax
import jax.numpy as jnp
from jax import lax
from jax.experimental import pallas as pl
from jax.experimental.pallas import tpu as pltpu
from jax.sharding import PartitionSpec as P

F32 = jnp.float32
BF16 = jnp.bfloat16
HIGHEST = lax.Precision.HIGHEST
MESH = pl.DeviceIdType.MESH
N = 512
R = 128
NX = 32
NY = 16
BLOCKS = [(a, b) for a in range(4) for b in range(a, 4)]
NZ = NX // 2
GROUP = 2 * NY
TILES = 160
PER = TILES // GROUP
VMEM_LIMIT = 48 * 1024 * 1024


def tree_sum(terms):
    while len(terms) > 1:
        terms = [
            terms[i] + terms[i + 1] if i + 1 < len(terms) else terms[i]
            for i in range(0, len(terms), 2)
        ]
    return terms[0]


def factor_inverse(gram):
    width = 16
    parts = width // 8
    row = lax.broadcasted_iota(jnp.int32, (R, R), 0)
    column = lax.broadcasted_iota(jnp.int32, (R, R), 1)
    diagonal = jnp.where(row == column, gram, 0.0)
    scale_rows = lax.rsqrt(jnp.sum(diagonal, axis=1, keepdims=True))
    scale_columns = lax.rsqrt(jnp.sum(diagonal, axis=0, keepdims=True))
    scaled = gram * scale_rows * scale_columns
    held = [scaled[8 * i : 8 * i + 8, :] for i in range(R // 8)]
    lane = lax.broadcasted_iota(jnp.int32, (8, R), 1)
    sub = lax.broadcasted_iota(jnp.int32, (8, R), 0)

    def along_lanes(x, l):
        return jnp.broadcast_to(x[:, l : l + 1], (8, R))

    def along_subs(x, s):
        return jnp.broadcast_to(x[s : s + 1, :], (8, R))

    out = []
    for k in range(R // width):
        base = k * width
        panel = [held[k * parts + t] for t in range(parts)]
        cols = [[along_lanes(panel[t], base + q) for t in range(parts)] for q in range(width)]
        panel = [
            jnp.where(lane == base + 8 * t + sub, panel[t] + 1.0, panel[t]) for t in range(parts)
        ]
        rows = []
        for j in range(width):
            tj, sj = divmod(j, 8)
            pivot = along_subs(cols[j][tj], sj)
            inverse = 1.0 / pivot
            pivot_row = along_subs(panel[tj], sj)
            kept = jnp.where(lane < base + j, pivot_row, jnp.where(lane == base + j, 1.0, 0.0))
            rows.append(kept * lax.rsqrt(pivot))
            factor = cols[j]
            pivot_row = pivot_row * inverse
            for t in range(parts):
                new = panel[t] - factor[t] * pivot_row
                panel[t] = jnp.where(sub == sj, pivot_row, new) if t == tj else new
            for q in range(j + 1, width):
                entry = along_subs(cols[q][tj], sj) * inverse
                for t in range(parts):
                    new = cols[q][t] - factor[t] * entry
                    cols[q][t] = jnp.where(sub == sj, entry, new) if t == tj else new
        for t in range(parts):
            block = rows[8 * t]
            for s in range(1, 8):
                block = jnp.where(sub >= s, rows[8 * t + s], block)
            out.append(block)
        spread = [along_subs(panel[q // 8], q % 8) for q in range(width)]
        for i in range((k + 1) * parts, R // 8):
            x = held[i]
            held[i] = x - tree_sum([along_lanes(x, base + q) * spread[q] for q in range(width)])
    return jnp.concatenate(out, axis=0) * scale_columns


def dot_tn(a, b, precision=None):
    return lax.dot_general(
        a, b, (((0,), (0,)), ((), ())), precision=precision, preferred_element_type=F32
    )


def dot_nt(a, b, precision=None):
    return lax.dot_general(
        a, b, (((1,), (1,)), ((), ())), precision=precision, preferred_element_type=F32
    )


def orth_pass(y_ref):
    y = y_ref[...]
    y_ref[...] = dot_nt(y, factor_inverse(dot_tn(y, y, HIGHEST)), HIGHEST)


def apply_gram(gram_ref, y_ref):
    y_ref[...] = jnp.dot(gram_ref[...], y_ref[...], precision=HIGHEST, preferred_element_type=F32)


def passes(count, gram_ref, y_ref):
    def step(t, carry):
        if gram_ref is not None:

            @pl.when(lax.rem(t, 2) == 0)
            def _():
                apply_gram(gram_ref, y_ref)

        orth_pass(y_ref)
        return carry

    lax.fori_loop(0, count, step, 0)


def remote(src, dst, send, recv, device):
    return pltpu.make_async_remote_copy(
        src_ref=src,
        dst_ref=dst,
        send_sem=send,
        recv_sem=recv,
        device_id=device,
        device_id_type=MESH,
    )


def wait_bytes(ref, sem):
    pltpu.make_async_copy(ref, ref, sem).wait()


class Place:
    def __init__(self):
        self.gx = lax.axis_index("gx")
        self.gy = lax.axis_index("gy")
        self.z = lax.div(self.gx, 2)
        self.core = lax.rem(self.gx, 2)
        self.member = 2 * self.gy + self.core

    def mate(self, d):
        member = lax.rem(self.member + d, GROUP)
        return member, (2 * self.z + lax.rem(member, 2), lax.div(member, 2))

    def line(self, d):
        return (2 * lax.rem(self.z + d, NZ) + self.core, self.gy)

    def crossed(self, d):
        return (2 * lax.rem(self.z + d, NZ) + 1 - self.core, self.gy)


def enter(place):
    barrier = pltpu.get_barrier_semaphore()

    def greet_mate(d, carry):
        _, device = place.mate(d)
        pl.semaphore_signal(barrier, inc=1, device_id=device, device_id_type=MESH)
        return carry

    def greet_line(d, carry):
        for device in (place.line(d), place.crossed(d)):
            pl.semaphore_signal(barrier, inc=1, device_id=device, device_id_type=MESH)
        return carry

    lax.fori_loop(1, GROUP, greet_mate, 0)
    lax.fori_loop(1, NZ, greet_line, 0)
    pl.semaphore_wait(barrier, GROUP - 1 + 2 * (NZ - 1))


def sum_all(place, bufs, during_plane=None, during_line=None):
    tiles, plane_in, line_out, line_in, piece, full, sent, plane_sems, line_sems, back_sem = bufs

    def send_plane(d, carry):
        member, device = place.mate(d)
        for c in range(PER):
            remote(
                tiles.at[member * PER + c],
                plane_in.at[c, place.member],
                sent.at[0],
                plane_sems.at[c],
                device,
            ).start()
        return carry

    lax.fori_loop(1, GROUP, send_plane, 0)
    if during_plane is not None:
        during_plane()
    for c in range(PER):
        plane_in[c, place.member] = tiles[place.member * PER + c]
        wait_bytes(plane_in.at[c, pl.ds(0, GROUP - 1)], plane_sems.at[c])
        part = tree_sum([plane_in[c, p] for p in range(GROUP)])
        line_out[c] = part
        line_in[c, place.z] = part

        def send_line(d, carry):
            remote(
                line_out.at[c],
                line_in.at[c, place.z],
                sent.at[1],
                line_sems.at[c],
                place.line(lax.rem(d + NZ // 2 - 1, NZ - 1) + 1),
            ).start()
            return carry

        lax.fori_loop(0, NZ - 1, send_line, 0)
    if during_line is not None:
        during_line()
    for c in range(PER):
        wait_bytes(line_in.at[c, pl.ds(0, NZ - 1)], line_sems.at[c])
        total = tree_sum([line_in[c, p] for p in range(NZ)])
        piece[c] = total
        full[place.member * PER + c] = total

        def send_back(d, carry):
            _, device = place.mate(d)
            remote(
                piece.at[c], full.at[place.member * PER + c], sent.at[2], back_sem, device
            ).start()
            return carry

        lax.fori_loop(1, GROUP, send_back, 0)
    wait_bytes(full.at[pl.ds(0, TILES - PER)], back_sem)
    wait_bytes(full.at[pl.ds(0, TILES - PER)], sent.at[0])
    wait_bytes(full.at[pl.ds(0, PER * (NZ - 1))], sent.at[1])
    wait_bytes(full.at[pl.ds(0, TILES - PER)], sent.at[2])


SUM_SCRATCH = [
    pltpu.VMEM((TILES, 8, R), F32),
    pltpu.VMEM((PER, GROUP, 8, R), F32),
    pltpu.VMEM((PER, 8, R), F32),
    pltpu.VMEM((PER, NZ, 8, R), F32),
    pltpu.VMEM((PER, 8, R), F32),
    pltpu.VMEM((TILES, 8, R), F32),
    pltpu.SemaphoreType.DMA((3,)),
    pltpu.SemaphoreType.DMA((PER,)),
    pltpu.SemaphoreType.DMA((PER,)),
    pltpu.SemaphoreType.DMA,
]


def pack(tiles, a, strip):
    for b in range(a, 4):
        tiles[pl.ds(16 * BLOCKS.index((a, b)), 16)] = strip[
            :, (b - a) * R : (b - a + 1) * R
        ].reshape(16, 8, R)


def unpack(full, gram_ref):
    for index, (a, b) in enumerate(BLOCKS):
        block = full[pl.ds(16 * index, 16)].reshape(R, R)
        gram_ref[pl.ds(a * R, R), pl.ds(b * R, R)] = block
        if a != b:
            gram_ref[pl.ds(b * R, R), pl.ds(a * R, R)] = block.T


def main_kernel(x_ref, start_one_ref, start_two_ref, basis_ref, held_two_ref, gram_two_ref, flat_ref, *scratch):
    gram_ref, wide, out_slots, in_slots, move_sems = scratch[:5]
    first = scratch[5 : 5 + len(SUM_SCRATCH)]
    second = scratch[5 + len(SUM_SCRATCH) :]
    place = Place()

    for a in range(4):
        pack(first[0], a, dot_tn(x_ref[:, pl.ds(a * R, R)], x_ref[:, pl.ds(a * R, N - a * R)]))
    enter(place)
    basis_ref[...] = start_one_ref[...]
    sum_all(
        place,
        first,
        during_plane=lambda: orth_pass(basis_ref),
        during_line=lambda: orth_pass(basis_ref),
    )
    unpack(first[5], gram_ref)
    passes(3, gram_ref, basis_ref)

    narrow = basis_ref[...].astype(BF16)

    def project(i, carry):
        rows = pl.ds(pl.multiple_of(i * 192, 192), 192)
        wide[rows, :] = jnp.dot(x_ref[rows, :], narrow, preferred_element_type=F32)
        return carry

    lax.fori_loop(0, 16, project, 0)

    def fill(to):
        for k in range(3):
            for j in range(2):
                column = wide[pl.ds(k * 64 + to * 2 + j, 16, stride=192), :]
                out_slots[to, k * 2 + j] = column.astype(BF16)

    def regroup(d, carry):
        offset = NX // 2 + lax.div(d + 1, 2) * (2 * lax.rem(d, 2) - 1)
        to = lax.rem(place.gx + offset, NX)
        fill(to)
        remote(
            out_slots.at[to],
            in_slots.at[place.gx],
            move_sems.at[0],
            move_sems.at[1],
            (to, place.gy),
        ).start()
        return carry

    lax.fori_loop(0, NX - 1, regroup, 0)
    fill(place.gx)
    in_slots[place.gx] = out_slots[place.gx]

    y = basis_ref[...]
    last = factor_inverse(dot_tn(y, y, HIGHEST))
    basis_ref[...] = dot_nt(y, last, HIGHEST)
    row = lax.broadcasted_iota(jnp.int32, (R, R), 0)
    column = lax.broadcasted_iota(jnp.int32, (R, R), 1)
    change = (last - jnp.where(row == column, 1.0, 0.0)).astype(BF16)
    held_two_ref[...] = start_two_ref[...]
    passes(2, None, held_two_ref)

    wait_bytes(in_slots.at[pl.ds(0, NX - 1)], move_sems.at[1])
    wait_bytes(out_slots.at[pl.ds(0, NX - 1)], move_sems.at[0])
    for c in range(6):
        arrived = in_slots[:, c].reshape(N, R)
        fixed = arrived.astype(F32) + dot_nt(arrived, change)
        flat_ref[:, c] = fixed.astype(BF16).reshape(NX, 16, R)
    for a in range(4):
        strip = None
        for c in range(6):
            left = flat_ref[pl.ds(8 * a, 8), c].reshape(R, R)
            right = flat_ref[pl.ds(8 * a, NX - 8 * a), c].reshape(N - a * R, R)
            part = dot_nt(left, right)
            strip = part if strip is None else strip + part
        pack(second[0], a, strip)
    sum_all(place, second)
    unpack(second[5], gram_two_ref)


def last_kernel(gram_ref, held_ref, flat_ref, basis_ref, core_ref):
    basis_ref[...] = held_ref[...]
    passes(4, gram_ref, basis_ref)
    narrow = basis_ref[...].astype(BF16)
    for c in range(6):
        core_ref[c] = dot_tn(narrow, flat_ref[:, c].reshape(N, R)).astype(BF16)


def vmem(count):
    return [pl.BlockSpec(memory_space=pltpu.VMEM)] * count


def call(kernel, outs, inputs, scratch=(), collective=None):
    return pl.pallas_call(
        kernel,
        out_shape=[jax.ShapeDtypeStruct(shape, dtype) for shape, dtype in outs],
        in_specs=vmem(len(inputs)),
        out_specs=vmem(len(outs)),
        scratch_shapes=list(scratch),
        compiler_params=pltpu.CompilerParams(
            collective_id=collective,
            has_side_effects=collective is not None,
            vmem_limit_bytes=VMEM_LIMIT,
        ),
    )(*inputs)


def local(field, start_one, start_two):
    rows = field.transpose(0, 2, 1, 3).reshape(-1, N)
    basis_one, held_two, gram_two, flat_two = call(
        main_kernel,
        [((N, R), F32), ((N, R), F32), ((N, N), F32), ((NX, 6, 16, R), BF16)],
        [rows, start_one, start_two],
        [
            pltpu.VMEM((N, N), F32),
            pltpu.VMEM((3072, R), F32),
            pltpu.VMEM((NX, 6, 16, R), BF16),
            pltpu.VMEM((NX, 6, 16, R), BF16),
            pltpu.SemaphoreType.DMA((2,)),
        ]
        + SUM_SCRATCH
        + SUM_SCRATCH,
        0,
    )
    basis_two, core = call(
        last_kernel, [((N, R), F32), ((6, R, R), BF16)], [gram_two, held_two, flat_two]
    )
    core = core.reshape(3, 2, R, R).transpose(2, 1, 0, 3)
    return basis_one, basis_two, core


def solution(mesh):
    placed = (P("gx", None, "gy", None), P(), P())
    return jax.shard_map(
        local,
        mesh=mesh,
        in_specs=placed,
        out_specs=(P(), P(), P(None, "gx", "gy", None)),
        check_vma=False,
    )
```

time: 198 us -> 172 us (0.87)
  Pallas kernels: 195 us -> 166 us
  local copies, waits for them, and re-layouts: 2.78 us -> 5.36 us
    pallas_call x4 -> x2, Pallas kernels: 195 us -> 166 us  [call(): pl.pallas_call(kernel, out_shape=[jax.ShapeDtypeStruct(shape, dtype) for...]
    unnamed x8 -> x7, local copies, waits for them, and re-layouts: 1.9 us -> 4.48 us
where the time goes in v2:
time: 172 us
  Pallas kernels  166 us (97%)
  local copies, waits for them, and re-layouts  5.36 us (3%)
    pallas_call x2, Pallas kernels, call(): pl.pallas_call(kernel, out_shape=[jax.ShapeDtypeStruct(shape, dtype) for...  166 us
    unnamed x7, local copies, waits for them, and re-layouts  4.48 us

profile of v2, /device:TPU:1, one launch (start us, length us, event | category | flops | bytes accessed | tf_op | source)
XLA Modules:
  0.0 171.9 jit_solution(10937802990300578661)
XLA Ops:
  0.6 0.0 copy-start
  0.6 1.9 %copy-done = bf16[16,64,3,512]{3,1,2,0:T(8,128)(2,1)S(1)} copy-done((bf16[16,64,3,512]{3,1,2,0:T(8,128)(2,1)S(1)}, bf16[16,64,3,512]{3,1,2,0:T(8,128)(2,1)}, u32[]{:S(2)}) %copy-start) | copy-done | bytes 3145752
  2.5 0.0 copy-start.1
  2.5 0.9 copy-done.1
  3.5 0.0 copy-start.2
  3.5 0.9 copy-done.2
  4.4 145.0 %shard_map.58 = (f32[512,128]{1,0:T(8,128)S(1)}, f32[512,128]{1,0:T(8,128)S(1)}, f32[512,512]{1,0:T(8,128)S(1)}, bf16[32,6,16,128]{3,2,1,0:T(8,128)(2,1)S(1)}) custom-call(bf16[3072,512]{1,0:T(8,128)(2,1)S(1)} %bitcast.7, f32[512,128]{1,0:T(8,128)S(1)} %copy-done.1, f32[512,128]{1,0:T(8,128)S(1)} %copy-done.2), custom_call_target="tpu_custom_call" | custom-call | tf_op jit(solution)/shard_map/pallas_call | solution.py:357
  149.5 20.9 %shard_map.59 = (f32[512,128]{1,0:T(8,128)}, bf16[6,128,128]{2,1,0:T(8,128)(2,1)S(1)}) custom-call(f32[512,512]{1,0:T(8,128)S(1)} %get-tuple-element.10.gram_ref, f32[512,128]{1,0:T(8,128)S(1)} %get-tuple-element.11.held_ref, bf16[32,6,16,128]{3,2,1,0:T(8,128)(2,1)S(1)} %get-tuple-element.12.flat_ref), custom_call_target="tpu_custom_call" | custom-call | tf_op jit(solution)/shard_map/pallas_call | solution.py:357
  170.4 0.9 copy.8
  171.2 0.7 copy.10
Async XLA Ops:
  0.6 1.9 %copy-start = (bf16[16,64,3,512]{3,1,2,0:T(8,128)(2,1)S(1)}, bf16[16,64,3,512]{3,1,2,0:T(8,128)(2,1)}, u32[]{:S(2)}) copy-start(bf16[16,64,3,512]{3,1,2,0:T(8,128)(2,1)} %param.3) | copy-start | bytes 9437188
  2.5 0.9 copy-start.1
  3.5 0.9 copy-start.2

commit v3 on v2

--- a/solution.py
+++ b/solution.py
@@ -16,11 +16,12 @@
 NX = 32
 NY = 16
 BLOCKS = [(a, b) for a in range(4) for b in range(a, 4)]
-NZ = NX // 2
-GROUP = 2 * NY
 TILES = 160
-PER = TILES // GROUP
-VMEM_LIMIT = 48 * 1024 * 1024
+HALF = TILES // 2
+PER = HALF // NY
+ROWS = 3072
+CHUNK = ROWS // 4
+VMEM_LIMIT = 61 * 1024 * 1024
 
 
 def tree_sum(terms):
@@ -145,106 +146,123 @@
         self.gy = lax.axis_index("gy")
         self.z = lax.div(self.gx, 2)
         self.core = lax.rem(self.gx, 2)
-        self.member = 2 * self.gy + self.core
-
-    def mate(self, d):
-        member = lax.rem(self.member + d, GROUP)
-        return member, (2 * self.z + lax.rem(member, 2), lax.div(member, 2))
-
-    def line(self, d):
-        return (2 * lax.rem(self.z + d, NZ) + self.core, self.gy)
-
-    def crossed(self, d):
-        return (2 * lax.rem(self.z + d, NZ) + 1 - self.core, self.gy)
-
-
-def enter(place):
+        self.quad = lax.rem(self.z, 4)
+        self.stride = lax.div(self.z, 4)
+
+    def partner(self):
+        return (2 * self.z + 1 - self.core, self.gy)
+
+    def plane(self, d):
+        gy = lax.rem(self.gy + d, NY)
+        return gy, (self.gx, gy)
+
+    def in_quad(self, d):
+        return (2 * (4 * self.stride + lax.rem(self.quad + d, 4)) + self.core, self.gy)
+
+    def in_stride(self, d):
+        return (2 * (4 * lax.rem(self.stride + d, 4) + self.quad) + self.core, self.gy)
+
+
+def greet(place):
     barrier = pltpu.get_barrier_semaphore()
 
-    def greet_mate(d, carry):
-        _, device = place.mate(d)
+    def greet_line(d, carry):
+        device = (lax.rem(place.gx + NX // 2 + d, NX), place.gy)
+
+        @pl.when(d != NX // 2)
+        def _():
+            pl.semaphore_signal(barrier, inc=1, device_id=device, device_id_type=MESH)
+
+        return carry
+
+    def greet_plane(d, carry):
+        _, device = place.plane(d)
         pl.semaphore_signal(barrier, inc=1, device_id=device, device_id_type=MESH)
         return carry
 
-    def greet_line(d, carry):
-        for device in (place.line(d), place.crossed(d)):
-            pl.semaphore_signal(barrier, inc=1, device_id=device, device_id_type=MESH)
-        return carry
-
-    lax.fori_loop(1, GROUP, greet_mate, 0)
-    lax.fori_loop(1, NZ, greet_line, 0)
-    pl.semaphore_wait(barrier, GROUP - 1 + 2 * (NZ - 1))
+    lax.fori_loop(0, NX, greet_line, 0)
+    lax.fori_loop(1, NY, greet_plane, 0)
+    return barrier
 
 
 def sum_all(place, bufs, during_plane=None, during_line=None):
-    tiles, plane_in, line_out, line_in, piece, full, sent, plane_sems, line_sems, back_sem = bufs
+    tiles, core_in, plane_in, quad_out, quad_in, line_out, line_in, piece, full, sent, got = bufs
+    own = place.core * HALF
+    other = HALF - own
+
+    remote(tiles.at[pl.ds(other, HALF)], core_in, sent.at[0], got.at[0], place.partner()).start()
+    wait_bytes(core_in, got.at[0])
+    core_in[...] += tiles[pl.ds(own, HALF)]
 
     def send_plane(d, carry):
-        member, device = place.mate(d)
-        for c in range(PER):
-            remote(
-                tiles.at[member * PER + c],
-                plane_in.at[c, place.member],
-                sent.at[0],
-                plane_sems.at[c],
-                device,
-            ).start()
-        return carry
-
-    lax.fori_loop(1, GROUP, send_plane, 0)
+        gy, device = place.plane(d)
+        remote(
+            core_in.at[pl.ds(gy * PER, PER)], plane_in.at[place.gy], sent.at[1], got.at[1], device
+        ).start()
+        return carry
+
+    lax.fori_loop(1, NY, send_plane, 0)
+    plane_in[place.gy] = core_in[pl.ds(place.gy * PER, PER)]
     if during_plane is not None:
         during_plane()
-    for c in range(PER):
-        plane_in[c, place.member] = tiles[place.member * PER + c]
-        wait_bytes(plane_in.at[c, pl.ds(0, GROUP - 1)], plane_sems.at[c])
-        part = tree_sum([plane_in[c, p] for p in range(GROUP)])
-        line_out[c] = part
-        line_in[c, place.z] = part
-
-        def send_line(d, carry):
-            remote(
-                line_out.at[c],
-                line_in.at[c, place.z],
-                sent.at[1],
-                line_sems.at[c],
-                place.line(lax.rem(d + NZ // 2 - 1, NZ - 1) + 1),
-            ).start()
-            return carry
-
-        lax.fori_loop(0, NZ - 1, send_line, 0)
+    wait_bytes(plane_in.at[pl.ds(0, NY - 1)], got.at[1])
+
+    part = tree_sum([plane_in[p] for p in range(NY)])
+    quad_out[...] = part
+    quad_in[place.quad] = part
+    for d in (2, 1, 3):
+        remote(
+            quad_out, quad_in.at[place.quad], sent.at[2], got.at[2], place.in_quad(d)
+        ).start()
+    wait_bytes(quad_in.at[pl.ds(0, 3)], got.at[2])
+
+    part = tree_sum([quad_in[p] for p in range(4)])
+    line_out[...] = part
+    line_in[place.stride] = part
+    for d in (2, 1, 3):
+        remote(
+            line_out, line_in.at[place.stride], sent.at[3], got.at[3], place.in_stride(d)
+        ).start()
     if during_line is not None:
         during_line()
-    for c in range(PER):
-        wait_bytes(line_in.at[c, pl.ds(0, NZ - 1)], line_sems.at[c])
-        total = tree_sum([line_in[c, p] for p in range(NZ)])
-        piece[c] = total
-        full[place.member * PER + c] = total
-
-        def send_back(d, carry):
-            _, device = place.mate(d)
-            remote(
-                piece.at[c], full.at[place.member * PER + c], sent.at[2], back_sem, device
-            ).start()
-            return carry
-
-        lax.fori_loop(1, GROUP, send_back, 0)
-    wait_bytes(full.at[pl.ds(0, TILES - PER)], back_sem)
-    wait_bytes(full.at[pl.ds(0, TILES - PER)], sent.at[0])
-    wait_bytes(full.at[pl.ds(0, PER * (NZ - 1))], sent.at[1])
-    wait_bytes(full.at[pl.ds(0, TILES - PER)], sent.at[2])
+    wait_bytes(line_in.at[pl.ds(0, 3)], got.at[3])
+
+    total = tree_sum([line_in[p] for p in range(4)])
+    piece[...] = total
+    here = own + place.gy * PER
+
+    def send_back(d, carry):
+        _, device = place.plane(d)
+        remote(piece, full.at[pl.ds(here, PER)], sent.at[4], got.at[4], device).start()
+        return carry
+
+    lax.fori_loop(1, NY, send_back, 0)
+    full[pl.ds(here, PER)] = total
+    wait_bytes(full.at[pl.ds(0, HALF - PER)], got.at[4])
+    half = full.at[pl.ds(own, HALF)]
+    remote(half, half, sent.at[5], got.at[5], place.partner()).start()
+    wait_bytes(core_in, got.at[5])
+
+    wait_bytes(core_in, sent.at[0])
+    wait_bytes(full.at[pl.ds(0, HALF - PER)], sent.at[1])
+    wait_bytes(quad_in.at[pl.ds(0, 3)], sent.at[2])
+    wait_bytes(line_in.at[pl.ds(0, 3)], sent.at[3])
+    wait_bytes(full.at[pl.ds(0, HALF - PER)], sent.at[4])
+    wait_bytes(core_in, sent.at[5])
 
 
 SUM_SCRATCH = [
     pltpu.VMEM((TILES, 8, R), F32),
-    pltpu.VMEM((PER, GROUP, 8, R), F32),
+    pltpu.VMEM((HALF, 8, R), F32),
+    pltpu.VMEM((NY, PER, 8, R), F32),
     pltpu.VMEM((PER, 8, R), F32),
-    pltpu.VMEM((PER, NZ, 8, R), F32),
+    pltpu.VMEM((4, PER, 8, R), F32),
+    pltpu.VMEM((PER, 8, R), F32),
+    pltpu.VMEM((4, PER, 8, R), F32),
     pltpu.VMEM((PER, 8, R), F32),
     pltpu.VMEM((TILES, 8, R), F32),
-    pltpu.SemaphoreType.DMA((3,)),
-    pltpu.SemaphoreType.DMA((PER,)),
-    pltpu.SemaphoreType.DMA((PER,)),
-    pltpu.SemaphoreType.DMA,
+    pltpu.SemaphoreType.DMA((6,)),
+    pltpu.SemaphoreType.DMA((6,)),
 ]
 
 
@@ -263,23 +281,52 @@
             gram_ref[pl.ds(b * R, R), pl.ds(a * R, R)] = block.T
 
 
-def main_kernel(x_ref, start_one_ref, start_two_ref, basis_ref, held_two_ref, gram_two_ref, flat_ref, *scratch):
-    gram_ref, wide, out_slots, in_slots, move_sems = scratch[:5]
-    first = scratch[5 : 5 + len(SUM_SCRATCH)]
-    second = scratch[5 + len(SUM_SCRATCH) :]
+def main_kernel(
+    field_ref,
+    start_one_ref,
+    start_two_ref,
+    basis_out,
+    held_two_out,
+    packed_out,
+    flat_out,
+    *scratch,
+):
+    (x_ref, gram_ref, wide, out_slots, in_slots, basis_ref, held_two_ref, flat_ref) = scratch[:8]
+    load_sems, move_sems, store_sems = scratch[8:11]
+    first = scratch[11 : 11 + len(SUM_SCRATCH)]
+    second = scratch[11 + len(SUM_SCRATCH) :]
     place = Place()
 
+    loads = [
+        pltpu.make_async_copy(
+            field_ref.at[pl.ds(q * CHUNK, CHUNK)], x_ref.at[pl.ds(q * CHUNK, CHUNK)], load_sems.at[q]
+        )
+        for q in range(4)
+    ]
+    loads.append(pltpu.make_async_copy(start_one_ref, basis_ref, load_sems.at[4]))
+    loads.append(pltpu.make_async_copy(start_two_ref, held_two_ref, load_sems.at[5]))
+    for load in loads:
+        load.start()
+    barrier = greet(place)
+    strips = [None] * 4
+    for q in range(4):
+        loads[q].wait()
+        rows = pl.ds(q * CHUNK, CHUNK)
+        for a in range(4):
+            part = dot_tn(x_ref[rows, pl.ds(a * R, R)], x_ref[rows, pl.ds(a * R, N - a * R)])
+            strips[a] = part if strips[a] is None else strips[a] + part
     for a in range(4):
-        pack(first[0], a, dot_tn(x_ref[:, pl.ds(a * R, R)], x_ref[:, pl.ds(a * R, N - a * R)]))
-    enter(place)
-    basis_ref[...] = start_one_ref[...]
+        pack(first[0], a, strips[a])
+    loads[4].wait()
+    loads[5].wait()
+    pl.semaphore_wait(barrier, NX + NY - 2)
     sum_all(
         place,
         first,
         during_plane=lambda: orth_pass(basis_ref),
         during_line=lambda: orth_pass(basis_ref),
     )
-    unpack(first[5], gram_ref)
+    unpack(first[8], gram_ref)
     passes(3, gram_ref, basis_ref)
 
     narrow = basis_ref[...].astype(BF16)
@@ -320,8 +367,11 @@
     row = lax.broadcasted_iota(jnp.int32, (R, R), 0)
     column = lax.broadcasted_iota(jnp.int32, (R, R), 1)
     change = (last - jnp.where(row == column, 1.0, 0.0)).astype(BF16)
-    held_two_ref[...] = start_two_ref[...]
+    stores = [pltpu.make_async_copy(basis_ref, basis_out, store_sems.at[0])]
+    stores[0].start()
     passes(2, None, held_two_ref)
+    stores.append(pltpu.make_async_copy(held_two_ref, held_two_out, store_sems.at[1]))
+    stores[1].start()
 
     wait_bytes(in_slots.at[pl.ds(0, NX - 1)], move_sems.at[1])
     wait_bytes(out_slots.at[pl.ds(0, NX - 1)], move_sems.at[0])
@@ -329,6 +379,8 @@
         arrived = in_slots[:, c].reshape(N, R)
         fixed = arrived.astype(F32) + dot_nt(arrived, change)
         flat_ref[:, c] = fixed.astype(BF16).reshape(NX, 16, R)
+    stores.append(pltpu.make_async_copy(flat_ref, flat_out, store_sems.at[2]))
+    stores[2].start()
     for a in range(4):
         strip = None
         for c in range(6):
@@ -338,27 +390,40 @@
             strip = part if strip is None else strip + part
         pack(second[0], a, strip)
     sum_all(place, second)
-    unpack(second[5], gram_two_ref)
-
-
-def last_kernel(gram_ref, held_ref, flat_ref, basis_ref, core_ref):
-    basis_ref[...] = held_ref[...]
+    stores.append(pltpu.make_async_copy(second[8], packed_out, store_sems.at[3]))
+    stores[3].start()
+    for store in stores:
+        store.wait()
+
+
+def last_kernel(
+    packed_in, held_in, flat_in, one_in, basis_ref, core_ref, one_out, packed, gram_ref, flat_ref, sems
+):
+    copies = [
+        pltpu.make_async_copy(source, target, sems.at[i])
+        for i, (source, target) in enumerate(
+            [(packed_in, packed), (held_in, basis_ref), (flat_in, flat_ref), (one_in, one_out)]
+        )
+    ]
+    for copy in copies:
+        copy.start()
+    copies[0].wait()
+    unpack(packed, gram_ref)
+    copies[1].wait()
     passes(4, gram_ref, basis_ref)
     narrow = basis_ref[...].astype(BF16)
+    copies[2].wait()
     for c in range(6):
         core_ref[c] = dot_tn(narrow, flat_ref[:, c].reshape(N, R)).astype(BF16)
-
-
-def vmem(count):
-    return [pl.BlockSpec(memory_space=pltpu.VMEM)] * count
-
-
-def call(kernel, outs, inputs, scratch=(), collective=None):
+    copies[3].wait()
+
+
+def call(kernel, ins, outs, inputs, scratch=(), collective=None):
     return pl.pallas_call(
         kernel,
-        out_shape=[jax.ShapeDtypeStruct(shape, dtype) for shape, dtype in outs],
-        in_specs=vmem(len(inputs)),
-        out_specs=vmem(len(outs)),
+        out_shape=[jax.ShapeDtypeStruct(shape, dtype) for shape, dtype, _ in outs],
+        in_specs=[pl.BlockSpec(memory_space=space) for space in ins],
+        out_specs=[pl.BlockSpec(memory_space=space) for _, _, space in outs],
         scratch_shapes=list(scratch),
         compiler_params=pltpu.CompilerParams(
             collective_id=collective,
@@ -370,23 +435,45 @@
 
 def local(field, start_one, start_two):
     rows = field.transpose(0, 2, 1, 3).reshape(-1, N)
-    basis_one, held_two, gram_two, flat_two = call(
+    hbm, vmem = pltpu.HBM, pltpu.VMEM
+    held_one, held_two, packed_two, flat_two = call(
         main_kernel,
-        [((N, R), F32), ((N, R), F32), ((N, N), F32), ((NX, 6, 16, R), BF16)],
+        [hbm] * 3,
+        [
+            ((N, R), F32, hbm),
+            ((N, R), F32, hbm),
+            ((TILES, 8, R), F32, hbm),
+            ((NX, 6, 16, R), BF16, hbm),
+        ],
         [rows, start_one, start_two],
         [
+            pltpu.VMEM((ROWS, N), BF16),
             pltpu.VMEM((N, N), F32),
-            pltpu.VMEM((3072, R), F32),
+            pltpu.VMEM((ROWS, R), F32),
             pltpu.VMEM((NX, 6, 16, R), BF16),
             pltpu.VMEM((NX, 6, 16, R), BF16),
+            pltpu.VMEM((N, R), F32),
+            pltpu.VMEM((N, R), F32),
+            pltpu.VMEM((NX, 6, 16, R), BF16),
+            pltpu.SemaphoreType.DMA((6,)),
             pltpu.SemaphoreType.DMA((2,)),
+            pltpu.SemaphoreType.DMA((4,)),
         ]
         + SUM_SCRATCH
         + SUM_SCRATCH,
         0,
     )
-    basis_two, core = call(
-        last_kernel, [((N, R), F32), ((6, R, R), BF16)], [gram_two, held_two, flat_two]
+    basis_two, core, basis_one = call(
+        last_kernel,
+        [hbm] * 4,
+        [((N, R), F32, vmem), ((6, R, R), BF16, vmem), ((N, R), F32, hbm)],
+        [packed_two, held_two, flat_two, held_one],
+        [
+            pltpu.VMEM((TILES, 8, R), F32),
+            pltpu.VMEM((N, N), F32),
+            pltpu.VMEM((NX, 6, 16, R), BF16),
+            pltpu.SemaphoreType.DMA((4,)),
+        ],
     )
     core = core.reshape(3, 2, R, R).transpose(2, 1, 0, 3)
     return basis_one, basis_two, core

time: 172 us -> 154 us (0.90)
  Pallas kernels: 166 us -> 151 us
  local copies, waits for them, and re-layouts: 5.36 us -> 1.81 us
    pallas_call x2, Pallas kernels: 166 us -> 151 us  [call(): pl.pallas_call(kernel, out_shape=[jax.ShapeDtypeStruct(shape, dtype) for...]
    unnamed x7 -> x0, local copies, waits for them, and re-layouts: 4.48 us -> none
where the time goes in v3:
time: 154 us
  Pallas kernels  151 us (98%)
  local copies, waits for them, and re-layouts  1.81 us (1%)
    pallas_call x2, Pallas kernels, call(): pl.pallas_call(kernel, out_shape=[jax.ShapeDtypeStruct(shape, dtype) for...  151 us

profile of v3, /device:TPU:1, one launch (start us, length us, event | category | flops | bytes accessed | tf_op | source)
XLA Modules:
  0.0 153.6 jit_solution(1097352252283116558)
XLA Ops:
  0.6 128.5 %shard_map.58 = (f32[512,128]{1,0:T(8,128)}, f32[512,128]{1,0:T(8,128)}, f32[160,8,128]{2,1,0:T(8,128)}, bf16[32,6,16,128]{3,2,1,0:T(8,128)(2,1)}) custom-call(bf16[3072,512]{1,0:T(8,128)(2,1)} %bitcast.7, f32[512,128]{1,0:T(8,128)} %start_one_ref.1, f32[512,128]{1,0:T(8,128)} %start_two_ref.1), custom_call_target="tpu_custom_call" | custom-call | tf_op jit(solution)/shard_map/pallas_call | solution.py:422
  129.2 22.6 %shard_map.59 = (f32[512,128]{1,0:T(8,128)}, bf16[6,128,128]{2,1,0:T(8,128)(2,1)}, f32[512,128]{1,0:T(8,128)}) custom-call(f32[160,8,128]{2,1,0:T(8,128)} %get-tuple-element.10.packed_in, f32[512,128]{1,0:T(8,128)} %get-tuple-element.11.held_in, bf16[32,6,16,128]{3,2,1,0:T(8,128)(2,1)} %get-tuple-element.12.flat_in, f32[512,128]{1,0:T(8,128)} %get-tuple-element.13.one_in), custom_call_target="tpu_custom_call" | custom-call | tf_op jit(solution)/shard_map/pallas_call | solution.py:422
  151.8 1.8 %copy.8 = bf16[3,2,128,128]{3,1,0,2:T(2,128)(2,1)} copy(bf16[3,2,128,128]{3,2,1,0:T(8,128)(2,1)} %bitcast.8) | data formatting | bytes 393216 | tf_op jit(solution)/shard_map/reshape | solution.py:478

commit v4 on v3

--- a/solution.py
+++ b/solution.py
@@ -19,9 +19,9 @@
 TILES = 160
 HALF = TILES // 2
 PER = HALF // NY
+CUTS = ((0, 3), (3, 2))
 ROWS = 3072
 CHUNK = ROWS // 4
-VMEM_LIMIT = 61 * 1024 * 1024
 
 
 def tree_sum(terms):
@@ -31,6 +31,30 @@
             for i in range(0, len(terms), 2)
         ]
     return terms[0]
+
+
+def split(x):
+    high = x.astype(BF16)
+    left = x - high.astype(F32)
+    middle = left.astype(BF16)
+    return high, middle, (left - middle.astype(F32)).astype(BF16)
+
+
+def product(x, y):
+    pair = jnp.concatenate([y[0], y[1]], axis=1)
+    top = dot_nn(x[0], pair)
+    second = dot_nn(x[1], pair)
+    third = dot_nn(
+        jnp.concatenate([x[0], x[2]], axis=1), jnp.concatenate([y[2], y[0]], axis=0)
+    )
+    return top[:, :R] + (top[:, R:] + second[:, :R] + (second[:, R:] + third))
+
+
+def gram_of(y):
+    high, middle, low = split(y)
+    top = dot_tn(high, jnp.concatenate([high, middle], axis=1))
+    cross = top[:, R:] + dot_tn(high, low)
+    return top[:, :R] + (cross + cross.T + dot_tn(middle, middle))
 
 
 def factor_inverse(gram):
@@ -57,6 +81,9 @@
         base = k * width
         panel = [held[k * parts + t] for t in range(parts)]
         cols = [[along_lanes(panel[t], base + q) for t in range(parts)] for q in range(width)]
+        after = range((k + 1) * parts, min((k + 2) * parts, R // 8))
+        rest = range((k + 2) * parts, R // 8)
+        after_cols = {i: [along_lanes(held[i], base + q) for q in range(width)] for i in after}
         panel = [
             jnp.where(lane == base + 8 * t + sub, panel[t] + 1.0, panel[t]) for t in range(parts)
         ]
@@ -83,11 +110,26 @@
             for s in range(1, 8):
                 block = jnp.where(sub >= s, rows[8 * t + s], block)
             out.append(block)
+        if not after:
+            break
         spread = [along_subs(panel[q // 8], q % 8) for q in range(width)]
-        for i in range((k + 1) * parts, R // 8):
-            x = held[i]
-            held[i] = x - tree_sum([along_lanes(x, base + q) * spread[q] for q in range(width)])
+        for i in after:
+            held[i] = held[i] - tree_sum([after_cols[i][q] * spread[q] for q in range(width)])
+        if rest:
+            x = split(jnp.concatenate([held[i] for i in rest], axis=0))
+            y = []
+            for part in split(jnp.concatenate(panel, axis=0)):
+                above = [jnp.zeros((base, R), BF16)] if base else []
+                below = [jnp.zeros((R - base - width, R), BF16)]
+                y.append(jnp.concatenate(above + [part] + below, axis=0))
+            change = product(x, y)
+            for t, i in enumerate(rest):
+                held[i] = held[i] - change[8 * t : 8 * t + 8]
     return jnp.concatenate(out, axis=0) * scale_columns
+
+
+def dot_nn(a, b):
+    return jnp.dot(a, b, preferred_element_type=F32)
 
 
 def dot_tn(a, b, precision=None):
@@ -104,11 +146,11 @@
 
 def orth_pass(y_ref):
     y = y_ref[...]
-    y_ref[...] = dot_nt(y, factor_inverse(dot_tn(y, y, HIGHEST)), HIGHEST)
+    y_ref[...] = dot_nt(y, factor_inverse(gram_of(y)), HIGHEST)
 
 
 def apply_gram(gram_ref, y_ref):
-    y_ref[...] = jnp.dot(gram_ref[...], y_ref[...], precision=HIGHEST, preferred_element_type=F32)
+    y_ref[...] = product([gram_ref[i] for i in range(3)], split(y_ref[...]))
 
 
 def passes(count, gram_ref, y_ref):
@@ -187,98 +229,135 @@
 
 def sum_all(place, bufs, during_plane=None, during_line=None):
     tiles, core_in, plane_in, quad_out, quad_in, line_out, line_in, piece, full, sent, got = bufs
-    own = place.core * HALF
-    other = HALF - own
-
-    remote(tiles.at[pl.ds(other, HALF)], core_in, sent.at[0], got.at[0], place.partner()).start()
-    wait_bytes(core_in, got.at[0])
-    core_in[...] += tiles[pl.ds(own, HALF)]
-
-    def send_plane(d, carry):
-        gy, device = place.plane(d)
+    own = place.core * NY
+    other = NY - own
+
+    def part_of(ref, h, *index):
+        return ref.at[(*index, pl.ds(*CUTS[h]))]
+
+    for h in range(2):
         remote(
-            core_in.at[pl.ds(gy * PER, PER)], plane_in.at[place.gy], sent.at[1], got.at[1], device
+            part_of(tiles, h, pl.ds(other, NY)),
+            part_of(core_in, h, pl.ds(0, NY)),
+            sent.at[0],
+            got.at[0, h],
+            place.partner(),
         ).start()
-        return carry
-
-    lax.fori_loop(1, NY, send_plane, 0)
-    plane_in[place.gy] = core_in[pl.ds(place.gy * PER, PER)]
+    for h in range(2):
+        span = pl.ds(*CUTS[h])
+        wait_bytes(part_of(core_in, h, pl.ds(0, NY)), got.at[0, h])
+        core_in[:, span] += tiles[pl.ds(own, NY), span]
+
+        def send_plane(d, carry):
+            gy, device = place.plane(d)
+            remote(
+                part_of(core_in, h, gy),
+                part_of(plane_in, h, place.gy),
+                sent.at[1],
+                got.at[1, h],
+                device,
+            ).start()
+            return carry
+
+        lax.fori_loop(1, NY, send_plane, 0)
+        plane_in[place.gy, span] = core_in[place.gy, span]
     if during_plane is not None:
         during_plane()
-    wait_bytes(plane_in.at[pl.ds(0, NY - 1)], got.at[1])
-
-    part = tree_sum([plane_in[p] for p in range(NY)])
-    quad_out[...] = part
-    quad_in[place.quad] = part
-    for d in (2, 1, 3):
-        remote(
-            quad_out, quad_in.at[place.quad], sent.at[2], got.at[2], place.in_quad(d)
-        ).start()
-    wait_bytes(quad_in.at[pl.ds(0, 3)], got.at[2])
-
-    part = tree_sum([quad_in[p] for p in range(4)])
-    line_out[...] = part
-    line_in[place.stride] = part
-    for d in (2, 1, 3):
-        remote(
-            line_out, line_in.at[place.stride], sent.at[3], got.at[3], place.in_stride(d)
-        ).start()
+    for h in range(2):
+        span = pl.ds(*CUTS[h])
+        wait_bytes(part_of(plane_in, h, pl.ds(0, NY - 1)), got.at[1, h])
+        part = tree_sum([plane_in[p, span] for p in range(NY)])
+        quad_out[span] = part
+        quad_in[place.quad, span] = part
+        for d in (2, 1, 3):
+            remote(
+                part_of(quad_out, h),
+                part_of(quad_in, h, place.quad),
+                sent.at[2],
+                got.at[2, h],
+                place.in_quad(d),
+            ).start()
+    for h in range(2):
+        span = pl.ds(*CUTS[h])
+        wait_bytes(part_of(quad_in, h, pl.ds(0, 3)), got.at[2, h])
+        part = tree_sum([quad_in[p, span] for p in range(4)])
+        line_out[span] = part
+        line_in[place.stride, span] = part
+        for d in (2, 1, 3):
+            remote(
+                part_of(line_out, h),
+                part_of(line_in, h, place.stride),
+                sent.at[3],
+                got.at[3, h],
+                place.in_stride(d),
+            ).start()
     if during_line is not None:
         during_line()
-    wait_bytes(line_in.at[pl.ds(0, 3)], got.at[3])
-
-    total = tree_sum([line_in[p] for p in range(4)])
-    piece[...] = total
-    here = own + place.gy * PER
-
-    def send_back(d, carry):
-        _, device = place.plane(d)
-        remote(piece, full.at[pl.ds(here, PER)], sent.at[4], got.at[4], device).start()
-        return carry
-
-    lax.fori_loop(1, NY, send_back, 0)
-    full[pl.ds(here, PER)] = total
-    wait_bytes(full.at[pl.ds(0, HALF - PER)], got.at[4])
-    half = full.at[pl.ds(own, HALF)]
-    remote(half, half, sent.at[5], got.at[5], place.partner()).start()
-    wait_bytes(core_in, got.at[5])
+    here = own + place.gy
+    for h in range(2):
+        span = pl.ds(*CUTS[h])
+        wait_bytes(part_of(line_in, h, pl.ds(0, 3)), got.at[3, h])
+        total = tree_sum([line_in[p, span] for p in range(4)])
+        piece[span] = total
+        full[here, span] = total
+
+        def send_back(d, carry):
+            _, device = place.plane(d)
+            remote(
+                part_of(piece, h), part_of(full, h, here), sent.at[4], got.at[4, h], device
+            ).start()
+            return carry
+
+        lax.fori_loop(1, NY, send_back, 0)
+    for h in range(2):
+        wait_bytes(part_of(full, h, pl.ds(0, NY - 1)), got.at[4, h])
+        half = part_of(full, h, pl.ds(own, NY))
+        remote(half, half, sent.at[5], got.at[5, h], place.partner()).start()
+    for h in range(2):
+        wait_bytes(part_of(core_in, h, pl.ds(0, NY)), got.at[5, h])
 
     wait_bytes(core_in, sent.at[0])
-    wait_bytes(full.at[pl.ds(0, HALF - PER)], sent.at[1])
+    wait_bytes(core_in.at[pl.ds(0, NY - 1)], sent.at[1])
     wait_bytes(quad_in.at[pl.ds(0, 3)], sent.at[2])
     wait_bytes(line_in.at[pl.ds(0, 3)], sent.at[3])
-    wait_bytes(full.at[pl.ds(0, HALF - PER)], sent.at[4])
+    wait_bytes(core_in.at[pl.ds(0, NY - 1)], sent.at[4])
     wait_bytes(core_in, sent.at[5])
 
 
 SUM_SCRATCH = [
-    pltpu.VMEM((TILES, 8, R), F32),
-    pltpu.VMEM((HALF, 8, R), F32),
+    pltpu.VMEM((2 * NY, PER, 8, R), F32),
+    pltpu.VMEM((NY, PER, 8, R), F32),
     pltpu.VMEM((NY, PER, 8, R), F32),
     pltpu.VMEM((PER, 8, R), F32),
     pltpu.VMEM((4, PER, 8, R), F32),
     pltpu.VMEM((PER, 8, R), F32),
     pltpu.VMEM((4, PER, 8, R), F32),
     pltpu.VMEM((PER, 8, R), F32),
-    pltpu.VMEM((TILES, 8, R), F32),
+    pltpu.VMEM((2 * NY, PER, 8, R), F32),
     pltpu.SemaphoreType.DMA((6,)),
-    pltpu.SemaphoreType.DMA((6,)),
+    pltpu.SemaphoreType.DMA((6, 2)),
 ]
 
 
 def pack(tiles, a, strip):
     for b in range(a, 4):
-        tiles[pl.ds(16 * BLOCKS.index((a, b)), 16)] = strip[
-            :, (b - a) * R : (b - a + 1) * R
-        ].reshape(16, 8, R)
+        first = 16 * BLOCKS.index((a, b))
+        for t in range(16):
+            tiles[(first + t) // PER, (first + t) % PER] = strip[
+                8 * t : 8 * t + 8, (b - a) * R : (b - a + 1) * R
+            ]
 
 
 def unpack(full, gram_ref):
     for index, (a, b) in enumerate(BLOCKS):
-        block = full[pl.ds(16 * index, 16)].reshape(R, R)
-        gram_ref[pl.ds(a * R, R), pl.ds(b * R, R)] = block
+        block = jnp.concatenate(
+            [full[t // PER, t % PER] for t in range(16 * index, 16 * index + 16)], axis=0
+        )
+        for i, part in enumerate(split(block)):
+            gram_ref[i, pl.ds(a * R, R), pl.ds(b * R, R)] = part
         if a != b:
-            gram_ref[pl.ds(b * R, R), pl.ds(a * R, R)] = block.T
+            for i, part in enumerate(split(block.T)):
+                gram_ref[i, pl.ds(b * R, R), pl.ds(a * R, R)] = part
 
 
 def main_kernel(
@@ -331,12 +410,9 @@
 
     narrow = basis_ref[...].astype(BF16)
 
-    def project(i, carry):
-        rows = pl.ds(pl.multiple_of(i * 192, 192), 192)
-        wide[rows, :] = jnp.dot(x_ref[rows, :], narrow, preferred_element_type=F32)
-        return carry
-
-    lax.fori_loop(0, 16, project, 0)
+    for q in range(4):
+        rows = pl.ds(q * CHUNK, CHUNK)
+        wide[rows, :] = dot_nn(x_ref[rows, :], narrow)
 
     def fill(to):
         for k in range(3):
@@ -362,7 +438,7 @@
     in_slots[place.gx] = out_slots[place.gx]
 
     y = basis_ref[...]
-    last = factor_inverse(dot_tn(y, y, HIGHEST))
+    last = factor_inverse(gram_of(y))
     basis_ref[...] = dot_nt(y, last, HIGHEST)
     row = lax.broadcasted_iota(jnp.int32, (R, R), 0)
     column = lax.broadcasted_iota(jnp.int32, (R, R), 1)
@@ -413,12 +489,13 @@
     passes(4, gram_ref, basis_ref)
     narrow = basis_ref[...].astype(BF16)
     copies[2].wait()
-    for c in range(6):
-        core_ref[c] = dot_tn(narrow, flat_ref[:, c].reshape(N, R)).astype(BF16)
+    for k in range(3):
+        pair = [dot_tn(narrow, flat_ref[:, 2 * k + j].reshape(N, R)) for j in range(2)]
+        core_ref[:, k] = jnp.stack(pair, axis=1).astype(BF16)
     copies[3].wait()
 
 
-def call(kernel, ins, outs, inputs, scratch=(), collective=None):
+def call(kernel, ins, outs, inputs, scratch, collective, limit):
     return pl.pallas_call(
         kernel,
         out_shape=[jax.ShapeDtypeStruct(shape, dtype) for shape, dtype, _ in outs],
@@ -428,7 +505,7 @@
         compiler_params=pltpu.CompilerParams(
             collective_id=collective,
             has_side_effects=collective is not None,
-            vmem_limit_bytes=VMEM_LIMIT,
+            vmem_limit_bytes=limit * 1024 * 1024,
         ),
     )(*inputs)
 
@@ -442,13 +519,13 @@
         [
             ((N, R), F32, hbm),
             ((N, R), F32, hbm),
-            ((TILES, 8, R), F32, hbm),
+            ((2 * NY, PER, 8, R), F32, hbm),
             ((NX, 6, 16, R), BF16, hbm),
         ],
         [rows, start_one, start_two],
         [
             pltpu.VMEM((ROWS, N), BF16),
-            pltpu.VMEM((N, N), F32),
+            pltpu.VMEM((3, N, N), BF16),
             pltpu.VMEM((ROWS, R), F32),
             pltpu.VMEM((NX, 6, 16, R), BF16),
             pltpu.VMEM((NX, 6, 16, R), BF16),
@@ -462,21 +539,23 @@
         + SUM_SCRATCH
         + SUM_SCRATCH,
         0,
+        61,
     )
     basis_two, core, basis_one = call(
         last_kernel,
         [hbm] * 4,
-        [((N, R), F32, vmem), ((6, R, R), BF16, vmem), ((N, R), F32, hbm)],
+        [((N, R), F32, vmem), ((R, 3, 2, R), BF16, vmem), ((N, R), F32, hbm)],
         [packed_two, held_two, flat_two, held_one],
         [
-            pltpu.VMEM((TILES, 8, R), F32),
-            pltpu.VMEM((N, N), F32),
+            pltpu.VMEM((2 * NY, PER, 8, R), F32),
+            pltpu.VMEM((3, N, N), BF16),
             pltpu.VMEM((NX, 6, 16, R), BF16),
             pltpu.SemaphoreType.DMA((4,)),
         ],
-    )
-    core = core.reshape(3, 2, R, R).transpose(2, 1, 0, 3)
-    return basis_one, basis_two, core
+        None,
+        61,
+    )
+    return basis_one, basis_two, core.transpose(0, 2, 1, 3)
 
 
 def solution(mesh):

time: 154 us -> 140 us (0.909)
  Pallas kernels: 151 us -> 139 us
  local copies, waits for them, and re-layouts: 1.81 us -> 0 us
    pallas_call x2, Pallas kernels: 151 us -> 139 us  [call(): pl.pallas_call(kernel, out_shape=[jax.ShapeDtypeStruct(shape, dtype) for...]
    reshape x1 -> x0, local copies, waits for them, and re-layouts: 1.81 us -> none  [local(): core = core.reshape(3, 2, R, R).transpose(2, 1, 0, 3)]
where the time goes in v4:
time: 140 us; the launch traced here: 139 us
  Pallas kernels  139 us (99%)
    pallas_call x2, Pallas kernels, call(): pl.pallas_call(kernel, out_shape=[jax.ShapeDtypeStruct(shape, dtype) for...  139 us

profile of v4, /device:TPU:1, one launch (start us, length us, event | category | flops | bytes accessed | tf_op | source)
XLA Modules:
  0.0 139.4 jit_solution(7038603297463225737)
XLA Ops:
  0.6 120.3 %shard_map.58 = (f32[512,128]{1,0:T(8,128)}, f32[512,128]{1,0:T(8,128)}, f32[32,5,8,128]{3,2,1,0:T(8,128)}, bf16[32,6,16,128]{3,2,1,0:T(8,128)(2,1)}) custom-call(bf16[3072,512]{1,0:T(8,128)(2,1)} %bitcast.4, f32[512,128]{1,0:T(8,128)} %start_one_ref.1, f32[512,128]{1,0:T(8,128)} %start_two_ref.1), custom_call_target="tpu_custom_call" | custom-call | tf_op jit(solution)/shard_map/pallas_call | solution.py:499
  121.0 18.3 %shard_map.59 = (f32[512,128]{1,0:T(8,128)}, bf16[128,3,2,128]{3,2,1,0:T(2,128)(2,1)}, f32[512,128]{1,0:T(8,128)}) custom-call(f32[32,5,8,128]{3,2,1,0:T(8,128)} %get-tuple-element.10.packed_in, f32[512,128]{1,0:T(8,128)} %get-tuple-element.11.held_in, bf16[32,6,16,128]{3,2,1,0:T(8,128)(2,1)} %get-tuple-element.12.flat_in, f32[512,128]{1,0:T(8,128)} %get-tuple-element.13.one_in), custom_call_target="tpu_custom_call" | custom-call | tf_op jit(solution)/shard_map/pallas_call | solution.py:499

commit v5 on v4

--- a/solution.py
+++ b/solution.py
@@ -191,6 +191,10 @@
         self.quad = lax.rem(self.z, 4)
         self.stride = lax.div(self.z, 4)
 
+    def far(self, d):
+        offset = NX // 2 + lax.div(d + 1, 2) * (2 * lax.rem(d, 2) - 1)
+        return lax.rem(self.gx + offset, NX)
+
     def partner(self):
         return (2 * self.z + 1 - self.core, self.gy)
 
@@ -227,7 +231,7 @@
     return barrier
 
 
-def sum_all(place, bufs, during_plane=None, during_line=None):
+def sum_all(place, bufs, during_plane=None, during_line=None, during_back=None):
     tiles, core_in, plane_in, quad_out, quad_in, line_out, line_in, piece, full, sent, got = bufs
     own = place.core * NY
     other = NY - own
@@ -309,6 +313,8 @@
             return carry
 
         lax.fori_loop(1, NY, send_back, 0)
+    if during_back is not None:
+        during_back()
     for h in range(2):
         wait_bytes(part_of(full, h, pl.ds(0, NY - 1)), got.at[4, h])
         half = part_of(full, h, pl.ds(own, NY))
@@ -371,9 +377,9 @@
     *scratch,
 ):
     (x_ref, gram_ref, wide, out_slots, in_slots, basis_ref, held_two_ref, flat_ref) = scratch[:8]
-    load_sems, move_sems, store_sems = scratch[8:11]
-    first = scratch[11 : 11 + len(SUM_SCRATCH)]
-    second = scratch[11 + len(SUM_SCRATCH) :]
+    raw, raw_out, raw_in, load_sems, move_sems, store_sems = scratch[8:14]
+    first = scratch[14 : 14 + len(SUM_SCRATCH)]
+    second = scratch[14 + len(SUM_SCRATCH) :]
     place = Place()
 
     loads = [
@@ -399,11 +405,49 @@
     loads[4].wait()
     loads[5].wait()
     pl.semaphore_wait(barrier, NX + NY - 2)
+
+    def gather_raw():
+        def widen(i, carry):
+            here = pl.ds(pl.multiple_of(i * 192 + 128, 64), 64)
+            there = pl.ds(pl.multiple_of(i * 64, 64), 64)
+            for l in range(4):
+                raw[l, there] = x_ref[here, pl.ds(l * R, R)].astype(F32)
+            return carry
+
+        def pick(to, carry):
+            for l in range(4):
+                rows = raw[l, pl.ds(2 * to + 1, 16, stride=64), :]
+                raw_out[to, :, pl.ds(l * R, R)] = rows.astype(BF16)
+            return carry
+
+        lax.fori_loop(0, 16, widen, 0)
+        lax.fori_loop(0, NX, pick, 0)
+        raw_in[place.gx] = raw_out[place.gx]
+
+    def during_line():
+        orth_pass(basis_ref)
+        gather_raw()
+
+    def move_raw():
+        def send(d, carry):
+            to = place.far(d)
+            remote(
+                raw_out.at[to],
+                raw_in.at[place.gx],
+                move_sems.at[2],
+                move_sems.at[3],
+                (to, place.gy),
+            ).start()
+            return carry
+
+        lax.fori_loop(0, NX - 1, send, 0)
+
     sum_all(
         place,
         first,
         during_plane=lambda: orth_pass(basis_ref),
-        during_line=lambda: orth_pass(basis_ref),
+        during_line=during_line,
+        during_back=move_raw,
     )
     unpack(first[8], gram_ref)
     passes(3, gram_ref, basis_ref)
@@ -415,14 +459,12 @@
         wide[rows, :] = dot_nn(x_ref[rows, :], narrow)
 
     def fill(to):
-        for k in range(3):
-            for j in range(2):
-                column = wide[pl.ds(k * 64 + to * 2 + j, 16, stride=192), :]
-                out_slots[to, k * 2 + j] = column.astype(BF16)
+        for c in range(5):
+            column = wide[pl.ds(c // 2 * 64 + to * 2 + c % 2, 16, stride=192), :]
+            out_slots[to, c] = column.astype(BF16)
 
     def regroup(d, carry):
-        offset = NX // 2 + lax.div(d + 1, 2) * (2 * lax.rem(d, 2) - 1)
-        to = lax.rem(place.gx + offset, NX)
+        to = place.far(d)
         fill(to)
         remote(
             out_slots.at[to],
@@ -449,10 +491,13 @@
     stores.append(pltpu.make_async_copy(held_two_ref, held_two_out, store_sems.at[1]))
     stores[1].start()
 
+    wait_bytes(raw_in.at[pl.ds(0, NX - 1)], move_sems.at[3])
+    wait_bytes(raw_out.at[pl.ds(0, NX - 1)], move_sems.at[2])
+    made_here = dot_nn(raw_in[...].reshape(N, N), narrow).astype(BF16)
     wait_bytes(in_slots.at[pl.ds(0, NX - 1)], move_sems.at[1])
     wait_bytes(out_slots.at[pl.ds(0, NX - 1)], move_sems.at[0])
     for c in range(6):
-        arrived = in_slots[:, c].reshape(N, R)
+        arrived = in_slots[:, c].reshape(N, R) if c < 5 else made_here
         fixed = arrived.astype(F32) + dot_nt(arrived, change)
         flat_ref[:, c] = fixed.astype(BF16).reshape(NX, 16, R)
     stores.append(pltpu.make_async_copy(flat_ref, flat_out, store_sems.at[2]))
@@ -527,13 +572,16 @@
             pltpu.VMEM((ROWS, N), BF16),
             pltpu.VMEM((3, N, N), BF16),
             pltpu.VMEM((ROWS, R), F32),
-            pltpu.VMEM((NX, 6, 16, R), BF16),
-            pltpu.VMEM((NX, 6, 16, R), BF16),
+            pltpu.VMEM((NX, 5, 16, R), BF16),
+            pltpu.VMEM((NX, 5, 16, R), BF16),
             pltpu.VMEM((N, R), F32),
             pltpu.VMEM((N, R), F32),
             pltpu.VMEM((NX, 6, 16, R), BF16),
+            pltpu.VMEM((4, 1024, R), F32),
+            pltpu.VMEM((NX, 16, N), BF16),
+            pltpu.VMEM((NX, 16, N), BF16),
             pltpu.SemaphoreType.DMA((6,)),
-            pltpu.SemaphoreType.DMA((2,)),
+            pltpu.SemaphoreType.DMA((4,)),
             pltpu.SemaphoreType.DMA((4,)),
         ]
         + SUM_SCRATCH

time: 140 us -> 135 us (0.964)
  Pallas kernels: 139 us -> 134 us
    pallas_call x2, Pallas kernels: 139 us -> 134 us  [call(): pl.pallas_call(kernel, out_shape=[jax.ShapeDtypeStruct(shape, dtype) for...]
where the time goes in v5:
time: 135 us
  Pallas kernels  134 us (99%)
    pallas_call x2, Pallas kernels, call(): pl.pallas_call(kernel, out_shape=[jax.ShapeDtypeStruct(shape, dtype) for...  134 us

profile of v5, /device:TPU:1, one launch (start us, length us, event | category | flops | bytes accessed | tf_op | source)
XLA Modules:
  0.0 134.9 jit_solution(10423054127116657437)
XLA Ops:
  0.6 115.8 %shard_map.58 = (f32[512,128]{1,0:T(8,128)}, f32[512,128]{1,0:T(8,128)}, f32[32,5,8,128]{3,2,1,0:T(8,128)}, bf16[32,6,16,128]{3,2,1,0:T(8,128)(2,1)}) custom-call(bf16[3072,512]{1,0:T(8,128)(2,1)} %bitcast.4, f32[512,128]{1,0:T(8,128)} %start_one_ref.1, f32[512,128]{1,0:T(8,128)} %start_two_ref.1), custom_call_target="tpu_custom_call" | custom-call | tf_op jit(solution)/shard_map/pallas_call | solution.py:544
  116.5 18.3 %shard_map.59 = (f32[512,128]{1,0:T(8,128)}, bf16[128,3,2,128]{3,2,1,0:T(2,128)(2,1)}, f32[512,128]{1,0:T(8,128)}) custom-call(f32[32,5,8,128]{3,2,1,0:T(8,128)} %get-tuple-element.10.packed_in, f32[512,128]{1,0:T(8,128)} %get-tuple-element.11.held_in, bf16[32,6,16,128]{3,2,1,0:T(8,128)(2,1)} %get-tuple-element.12.flat_in, f32[512,128]{1,0:T(8,128)} %get-tuple-element.13.one_in), custom_call_target="tpu_custom_call" | custom-call | tf_op jit(solution)/shard_map/pallas_call | solution.py:544

commit v6 on v5

--- a/solution.py
+++ b/solution.py
@@ -149,6 +149,33 @@
     y_ref[...] = dot_nt(y, factor_inverse(gram_of(y)), HIGHEST)
 
 
+def identity():
+    row = lax.broadcasted_iota(jnp.int32, (R, R), 0)
+    column = lax.broadcasted_iota(jnp.int32, (R, R), 1)
+    return jnp.where(row == column, 1.0, 0.0), row, column
+
+
+def second_pass(y_ref):
+    y = y_ref[...]
+    gram = gram_of(y)
+    one, row, column = identity()
+    weight = jnp.where(row > column, 1.0, 0.5 * one)
+    error = gram - one
+    size = jnp.sum(error * error)
+    near = size < 1e-6
+
+    @pl.when(near)
+    def _():
+        a = error * weight
+        narrow = a.astype(BF16)
+        second = dot_nn(narrow, narrow) + dot_nt(narrow, narrow) * weight
+        y_ref[...] = dot_nt(y, (one - a) + second, HIGHEST)
+
+    @pl.when(jnp.logical_not(near))
+    def _():
+        y_ref[...] = dot_nt(y, factor_inverse(gram), HIGHEST)
+
+
 def apply_gram(gram_ref, y_ref):
     y_ref[...] = product([gram_ref[i] for i in range(3)], split(y_ref[...]))
 
@@ -531,7 +558,14 @@
     copies[0].wait()
     unpack(packed, gram_ref)
     copies[1].wait()
-    passes(4, gram_ref, basis_ref)
+
+    def step(t, carry):
+        apply_gram(gram_ref, basis_ref)
+        orth_pass(basis_ref)
+        second_pass(basis_ref)
+        return carry
+
+    lax.fori_loop(0, 2, step, 0)
     narrow = basis_ref[...].astype(BF16)
     copies[2].wait()
     for k in range(3):

time: 135 us -> 131 us (0.970)
  Pallas kernels: 134 us -> 130 us
    pallas_call x2, Pallas kernels: 134 us -> 130 us  [call(): pl.pallas_call(kernel, out_shape=[jax.ShapeDtypeStruct(shape, dtype) for...]
where the time goes in v6:
time: 131 us
  Pallas kernels  130 us (99%)
    pallas_call x2, Pallas kernels, call(): pl.pallas_call(kernel, out_shape=[jax.ShapeDtypeStruct(shape, dtype) for...  130 us

profile of v6, /device:TPU:1, one launch (start us, length us, event | category | flops | bytes accessed | tf_op | source)
XLA Modules:
  0.0 131.2 jit_solution(15253406586306460211)
XLA Ops:
  0.6 115.8 %shard_map.58 = (f32[512,128]{1,0:T(8,128)}, f32[512,128]{1,0:T(8,128)}, f32[32,5,8,128]{3,2,1,0:T(8,128)}, bf16[32,6,16,128]{3,2,1,0:T(8,128)(2,1)}) custom-call(bf16[3072,512]{1,0:T(8,128)(2,1)} %bitcast.4, f32[512,128]{1,0:T(8,128)} %start_one_ref.1, f32[512,128]{1,0:T(8,128)} %start_two_ref.1), custom_call_target="tpu_custom_call" | custom-call | tf_op jit(solution)/shard_map/pallas_call | solution.py:578
  116.5 14.6 %shard_map.59 = (f32[512,128]{1,0:T(8,128)}, bf16[128,3,2,128]{3,2,1,0:T(2,128)(2,1)}, f32[512,128]{1,0:T(8,128)}) custom-call(f32[32,5,8,128]{3,2,1,0:T(8,128)} %get-tuple-element.10.packed_in, f32[512,128]{1,0:T(8,128)} %get-tuple-element.11.held_in, bf16[32,6,16,128]{3,2,1,0:T(8,128)(2,1)} %get-tuple-element.12.flat_in, f32[512,128]{1,0:T(8,128)} %get-tuple-element.13.one_in), custom_call_target="tpu_custom_call" | custom-call | tf_op jit(solution)/shard_map/pallas_call | solution.py:578
